TPU v7x, 32 devices: a whole 2x2x4 slice. The times are simulated.
32 devices in a mesh: groups: 2 (over x), row: 4 (over y, core), col: 4 (over z).
Axes of the slice: x: 2, y: 2, z: 4, core: 2. Of those that a mesh axis runs over, the one named last changes fastest.
Arguments:
- tokens: bfloat16 [1024, 8192], P(('groups', 'row'), 'col'), parts along dimension 0, may hold values from -6 to 6
- gate_weight: bfloat16 [8192, 16384], P('col', 'row'), may hold values from -0.09375 to 0.09375
- up_weight: bfloat16 [8192, 16384], P('col', 'row'), may hold values from -0.09375 to 0.09375
- down_weight: bfloat16 [16384, 8192], P('row', 'col'), may hold values from -0.09375 to 0.09375
- gate_mask: int32 [64, 128], P('col', 'row'), may hold values from 0 to 1, as said below
- up_mask: int32 [64, 128], P('col', 'row'), may hold values from 0 to 1, as said below
- down_mask: int32 [128, 64], P('row', 'col'), may hold values from 0 to 1, as said below
Outputs:
- mixed: bfloat16 [1024, 8192], P(('groups', 'row'), 'col'), parts along dimension 0
There are 2 independent parts, one for each index of `groups`. A program takes and returns all parts, laid end to end along the dimension named above; an argument that names none is the same for every part. Nothing has to cross between parts.
Inputs may be any that keep to these rules, and one draw needn't show every extreme that they name: `gate_mask`: 1 where a 128 x 128 tile of the gate projection is kept, else 0; the share kept differs from one block of 128 hidden units to another. `up_mask`: 1 where a tile of the up projection is kept, else 0. `down_mask`: 1 where a tile of the down projection is kept, else 0.
All inputs are finite; a program needn't handle non-finite values.
Results may differ from a plain program's by a relative error of at most 0.02.
Values may be sent and summed in bfloat16 or wider, within the bound.
No kernel may reach another device: no remote copies, remote signals or barrier semaphores. Data moves between devices by JAX's collectives and lax.ppermute only.
A program may use at most 256 MiB of HBM per device.

v0:
```python
import jax
import jax.numpy as jnp
from jax import lax
from jax.sharding import PartitionSpec as P


def pruned(weight, mask):
    tile_edge = weight.shape[0] // mask.shape[0]
    spread = jnp.repeat(jnp.repeat(mask, tile_edge, axis=0), tile_edge, axis=1)
    return weight * spread.astype(jnp.bfloat16)


def shards(tokens, gate_weight, up_weight, down_weight, gate_mask, up_mask, down_mask):
    gate_pruned = pruned(gate_weight, gate_mask)
    up_pruned = pruned(up_weight, up_mask)
    down_pruned = pruned(down_weight, down_mask)
    units = gate_weight.shape[1]
    both_pruned = jnp.concatenate([gate_pruned, up_pruned], axis=1)
    partial_value = jnp.dot(
        lax.all_gather(tokens, "row", axis=0, tiled=True),
        both_pruned,
        preferred_element_type=jnp.float32,
    )
    summed = lax.psum_scatter(
        partial_value.astype(jnp.bfloat16), "col", scatter_dimension=0, tiled=True
    ).astype(jnp.float32)
    hidden = (jax.nn.silu(summed[:, :units]) * summed[:, units:]).astype(jnp.bfloat16)
    terms = jnp.dot(
        lax.all_gather(hidden, "col", axis=0, tiled=True),
        down_pruned,
        preferred_element_type=jnp.float32,
    )
    return lax.psum_scatter(terms.astype(jnp.bfloat16), "row", scatter_dimension=0, tiled=True)


def solution(mesh):
    in_specs = (
        P(("groups", "row"), "col"),
        P("col", "row"),
        P("col", "row"),
        P("row", "col"),
        P("col", "row"),
        P("col", "row"),
        P("row", "col"),
    )
    out_specs = P(("groups", "row"), "col")
    return jax.shard_map(shards, mesh=mesh, in_specs=in_specs, out_specs=out_specs, check_vma=False)
```

profile of v0, /device:TPU:0, one launch (start us, length us, event | category | flops | bytes accessed | tf_op | source)
XLA Modules:
  0.0 421.7 jit_solution(8105700129489954900)
XLA Ops:
  6.5 0.0 all-gather.3.cloned.1.call-start
  6.5 0.7 all-gather.3.cloned.1.call-update
  7.3 0.0 reduce-scatter.7.cloned.1.call-start
  7.3 0.7 convert_element_type.48
  8.0 0.7 convert_element_type.51
  8.7 0.1 broadcast_in_dim.18
  8.8 25.4 %broadcast_in_dim.19 = bf16[2048,32,128]{2,1,0:T(8,128)(2,1)S(1)} broadcast(bf16[2048,32]{1,0:T(8,128)(2,1)S(1)} %bitcast.24), dimensions={0,1} | broadcast | bytes 16908288 | tf_op jit(solution)/shard_map/broadcast_in_dim | solution.py:9
  34.2 0.1 broadcast_in_dim.20
  34.3 15.8 %broadcast_in_dim.21 = bf16[2048,32,128]{2,1,0:T(8,128)(2,1)} broadcast(bf16[2048,32]{1,0:T(8,128)(2,1)S(1)} %bitcast.25), dimensions={0,1} | broadcast | bytes 16908288 | tf_op jit(solution)/shard_map/broadcast_in_dim | solution.py:9
  50.1 29.8 %bitcast_multiply_fusion.2 = (bf16[2048,4096]{1,0:T(8,128)(2,1)}, bf16[2048,4096]{1,0:T(8,128)(2,1)}) fusion(bf16[2048,4096]{1,0:T(8,128)(2,1)} %param.9, bf16[256,8,32,128]{3,2,1,0:T(8,128)(2,1)} %bitcast.21, bf16[2048,4096]{1,0:T(8,128)(2,1)} %param.8, bf16[256,8,32,128]{3,2,1,0:T(8,128)(2,1)S(1)} %bitcast.20), kind=kLoop, calls=%fused_computation.7 | loop fusion | flops 16777216 | bytes 100663296 | tf_op jit(solution)/shard_map/mul | solution.py:10
  79.9 0.0 all-gather.3.cloned.1.call-done
  79.9 24.9 %fusion.9 = bf16[512,8192]{0,1:T(8,128)(2,1)} fusion(bf16[512,2048]{1,0:T(8,128)(2,1)} %all-gather.3.cloned.1.call-done, bf16[2048,4096]{1,0:T(8,128)(2,1)} %get-tuple-element.5, bf16[2048,4096]{1,0:T(8,128)(2,1)} %get-tuple-element.6), kind=kOutput, calls=%fused_computation.10 | convolution fusion | flops 17251172352 | bytes 44040192 | tf_op jit(solution)/shard_map/dot_general | solution.py:19
  104.9 11.3 %copy.10 = bf16[512,8192]{1,0:T(8,128)(2,1)} copy(bf16[512,8192]{0,1:T(8,128)(2,1)} %fusion.9) | data formatting | bytes 16777216
  116.2 0.0 copy-start
  116.2 0.0 reduce-scatter.7.cloned.1.call-update
  116.2 0.0 all-gather.5.cloned.1.call-start
  116.3 147.3 %reduce-scatter.7.cloned.1.call-done = bf16[128,8192]{1,0:T(8,128)(2,1)} async-done(((bf16[512,8192]{1,0:T(8,128)(2,1)}), bf16[128,8192]{1,0:T(8,128)(2,1)}) %reduce-scatter.7.cloned.1.call-update) | async-done | bytes 2097168
  263.6 3.2 copy.11
  266.8 0.3 convert_element_type.56
  267.1 1.5 fusion.13
  268.6 0.0 all-gather.5.cloned.1.call-update
  268.6 0.2 reduce-scatter.5.cloned.1.call-start
  268.8 0.0 copy-done
  268.9 0.1 copy.9
  268.9 81.1 %all-gather.5.cloned.1.call-done = bf16[512,4096]{0,1:T(8,128)(2,1)} async-done(((bf16[128,4096]{0,1:T(8,128)(2,1)}), bf16[512,4096]{0,1:T(8,128)(2,1)}) %all-gather.5.cloned.1.call-update) | async-done | bytes 4194320 | tf_op jit(solution)/shard_map/all_gather | solution.py:29
  350.1 0.1 broadcast_in_dim.22
  350.2 0.0 copy-start.1
  350.2 18.9 %broadcast_in_dim.23 = bf16[4096,16,128]{2,1,0:T(8,128)(2,1)} broadcast(bf16[4096,16]{1,0:T(8,128)(2,1)S(1)} %bitcast.23), dimensions={0,1} | broadcast | bytes 16908288 | tf_op jit(solution)/shard_map/broadcast_in_dim | solution.py:9
  369.1 0.0 copy-done.1
  369.1 16.3 %fusion.12 = bf16[512,2048]{1,0:T(8,128)(2,1)} fusion(bf16[512,4096]{0,1:T(8,128)(2,1)S(1)} %copy-done.1, bf16[4096,2048]{1,0:T(8,128)(2,1)} %param.10, bf16[512,8,16,128]{3,2,1,0:T(8,128)(2,1)} %bitcast.22), kind=kOutput, calls=%fused_computation.11 | convolution fusion | flops 8599371776 | bytes 39845888 | tf_op jit(solution)/shard_map/dot_general | solution.py:28
  385.4 0.0 reduce-scatter.5.cloned.1.call-update
  385.4 29.8 %reduce-scatter.5.cloned.1.call-done = bf16[128,2048]{1,0:T(8,128)(2,1)} async-done(((bf16[512,2048]{1,0:T(8,128)(2,1)}), bf16[128,2048]{1,0:T(8,128)(2,1)}) %reduce-scatter.5.cloned.1.call-update) | async-done | bytes 524304 | tf_op jit(solution)/shard_map/reduce_scatter | solution.py:33
  (1 shorter events, 0.0 us)
Async XLA Ops:
  6.5 73.4 %all-gather.3.cloned.1.call-start = ((), (), s32[]{:S(2)}) async-start(), calls=%async_computation.2 | async-start | bytes 2621440 | tf_op jit(solution)/shard_map/all_gather | solution.py:20
  7.3 256.3 %reduce-scatter.7.cloned.1.call-start = ((), (), s32[]{:S(2)}) async-start(), calls=%async_computation.5 | async-start | bytes 10485760
  116.2 152.6 %copy-start = (s32[32,16]{0,1:T(8,128)S(1)}, s32[32,16]{0,1:T(8,128)}, u32[]{:S(2)}) copy-start(s32[32,16]{0,1:T(8,128)} %param.13) | copy-start | bytes 6148
  116.2 233.8 %all-gather.5.cloned.1.call-start = ((), (), s32[]{:S(2)}) async-start(), calls=%async_computation.3 | async-start | bytes 5242880 | tf_op jit(solution)/shard_map/all_gather | solution.py:29
  268.6 146.6 %reduce-scatter.5.cloned.1.call-start = ((), (), s32[]{:S(2)}) async-start(), calls=%async_computation.4 | async-start | bytes 2621440 | tf_op jit(solution)/shard_map/reduce_scatter | solution.py:33
  350.2 18.9 %copy-start.1 = (bf16[512,4096]{0,1:T(8,128)(2,1)S(1)}, bf16[512,4096]{0,1:T(8,128)(2,1)}, u32[]{:S(2)}) copy-start(bf16[512,4096]{0,1:T(8,128)(2,1)} %all-gather.5.cloned.1.call-done) | copy-start | bytes 12582916
Sparse Core Ops, SparseCore 0:
  8.9 25.2 all-gather.2
  116.4 147.1 reduce-scatter.6
  268.7 81.2 all-gather.4
  385.6 29.5 reduce-scatter.4
where the time goes:
time: 422 us
  waiting for transfers between devices  259 us (61%)
  local copies, waits for them, and re-layouts  75.1 us (18%)
  matrix products  41.2 us (10%)
  other arithmetic  33 us (8%)
  between operations  13.2 us (3%)
    unnamed x5, waiting for transfers between devices  148 us
    all_gather x1, waiting for transfers between devices, shards(): lax.all_gather(hidden, 'col', axis=0, tiled=True)  81.1 us
    broadcast_in_dim x6, local copies, waits for them, and re-layouts, pruned(): spread = jnp.repeat(jnp.repeat(mask, tile_edge, axis=0), tile_edge, axis=1)  60.4 us
    mul x1, other arithmetic, pruned(): return weight * spread.astype(jnp.bfloat16)  29.8 us
    reduce_scatter x1, waiting for transfers between devices, shards(): lax.psum_scatter(terms.astype(jnp.bfloat16), 'row', scatter_dimension=0,...  29.8 us
    dot_general x1, matrix products, shards(): jnp.dot(lax.all_gather(tokens, 'row', axis=0, tiled=True), both_pruned, p...  24.9 us
    dot_general x1, matrix products, shards(): jnp.dot(lax.all_gather(hidden, 'col', axis=0, tiled=True), down_pruned, p...  16.3 us
    unnamed x6, local copies, waits for them, and re-layouts  14.6 us
  transfers between devices with their start and end apart: 4, of which 3 were waited for; matrix products, arithmetic and copies ran while one was open for 17% of the time, Pallas kernels for 0%

commit v1 on v0

v1 whole, which is shorter than its diff:
```python
import functools

import jax
import jax.numpy as jnp
from jax import lax
from jax.experimental import pallas as pl
from jax.experimental.pallas import tpu as pltpu
from jax.sharding import PartitionSpec as P

LAG = 2
ANY = pl.BlockSpec(memory_space=pl.ANY)
SMEM = pl.BlockSpec(memory_space=pltpu.SMEM)
VMEM = pl.BlockSpec(memory_space=pltpu.VMEM)
MIB = 1 << 20


def masked(block, mask, row, col, edge):
    strips = []
    for i in range(block.shape[0] // edge):
        tiles = []
        for j in range(block.shape[1] // edge):
            keep = mask[row + i, col + j].astype(jnp.float32).astype(jnp.bfloat16)
            tiles.append(block[i * edge:(i + 1) * edge, j * edge:(j + 1) * edge] * keep)
        strips.append(jnp.concatenate(tiles, axis=1))
    return jnp.concatenate(strips, axis=0)


def partial_kernel(edge, cols, gm, um, tok, x, ga, ua, gb, ub, pa, pb, tok_out, acc):
    k, steps = pl.program_id(0), pl.num_programs(0)
    row = k * (ga.shape[0] // edge)
    units = ga.shape[1]

    @pl.when(k == 0)
    def _():
        acc[...] = jnp.zeros_like(acc)

    for i, (w, m, col) in enumerate(((ga, gm, cols[0]), (ua, um, cols[0]), (gb, gm, cols[1]), (ub, um, cols[1]))):
        acc[:, i * units:(i + 1) * units] += jnp.dot(
            x[...], masked(w, m, row, col, edge), preferred_element_type=jnp.float32
        )

    @pl.when(k == steps - 1)
    def _():
        pa[...] = acc[:, :2 * units].astype(pa.dtype)
        pb[...] = acc[:, 2 * units:].astype(pb.dtype)


def partials(tok, x, gate, up, gm, um, unit, units):
    rows, depth = x.shape
    edge = depth // gm.shape[0]
    block = min(512, depth)
    half = gate.shape[1] // 2 // units
    near = pl.BlockSpec((block, units), lambda k: (k, unit))
    far = pl.BlockSpec((block, units), lambda k: (k, half + unit))
    out = jax.ShapeDtypeStruct((rows, 2 * units), jnp.bfloat16)
    return pl.pallas_call(
        functools.partial(partial_kernel, edge, (unit * units // edge, (half + unit) * units // edge)),
        grid=(depth // block,),
        in_specs=[SMEM, SMEM, ANY, pl.BlockSpec((rows, block), lambda k: (0, k)), near, near, far, far],
        out_specs=[pl.BlockSpec((rows, 2 * units), lambda k: (0, 0))] * 2 + [ANY],
        out_shape=[out, out, jax.ShapeDtypeStruct(tok.shape, tok.dtype)],
        scratch_shapes=[pltpu.VMEM((rows, 4 * units), jnp.float32)],
        input_output_aliases={2: 2},
        compiler_params=pltpu.CompilerParams(vmem_limit_bytes=52 * MIB),
    )(gm, um, tok, x, gate, up, gate, up)


def swiglu(gate, up):
    return gate / (1.0 + jnp.exp(-gate)) * up


def hop_kernel(cols, step, lag, units, wide, sent, z_ref, tok, left_in, right_in, *rest):
    count = sum(len(c) for c in cols)
    own, (left_out, right_out, tok_out, a, b, sems) = rest[:count], rest[count:]
    own_a, own_b = own[:len(cols[0])], own[len(cols[0]):]
    z = z_ref[0]
    n_col = wide[2]
    span = 2 * units

    def each(act):
        for refs, where, to, sem in ((own_a, cols[0], a, 0), (own_b, cols[1], b, 1)):
            for ref, i in zip(refs, where):
                @pl.when(z == i)
                def _(ref=ref, to=to, sem=sem):
                    act(pltpu.make_async_copy(ref, to, sems.at[sem]))

    each(lambda c: c.start())
    if sent[1]:
        at = span if sent[0] else 0
        come = span
        if wide[1]:
            @pl.when(z > 0)
            def _():
                right_out[:, at:at + units] = right_in[:, come:come + units]

            @pl.when(z < n_col - 1)
            def _():
                left_out[:, at:at + units] = left_in[:, come:come + units]
    each(lambda c: c.wait())

    rows = a.shape[0]
    piece = min(16, rows)

    def over(body):
        def one(i, _):
            body(pl.ds(pl.multiple_of(i * piece, piece), piece))
            return 0
        lax.fori_loop(0, rows // piece, one, 0)

    for came, mine, goes, back, origin, end in (
        (left_in, a, left_out, right_out, n_col - 1, 0),
        (right_in, b, right_out, left_out, 0, n_col - 1),
    ):
        if sent[0]:
            @pl.when(z == origin)
            def _(mine=mine, goes=goes):
                goes[:, :span] = mine[...]

            @pl.when((z != origin) & (z != end))
            def _(came=came, mine=mine, goes=goes):
                def add(r):
                    goes[r, :span] = (came[r, :span].astype(jnp.float32) + mine[r, :].astype(jnp.float32)).astype(goes.dtype)
                over(add)
        if sent[1]:
            @pl.when(z == end)
            def _(came=came, mine=mine, back=back):
                def finish(r):
                    total = came[r, :span].astype(jnp.float32) + mine[r, :].astype(jnp.float32)
                    back[r, at:at + units] = swiglu(total[:, :units], total[:, units:]).astype(back.dtype)
                over(finish)


def hop(tok, z, left_in, right_in, own_a, own_b, step, lag, units, arrives, leaves, n_col):
    rows = left_in.shape[0]
    width = (2 * units if leaves[0] else 0) + (units if leaves[1] else 0)
    out = jax.ShapeDtypeStruct((rows, width), jnp.bfloat16)
    cols = (tuple(i for i, _ in own_a), tuple(i for i, _ in own_b))
    return pl.pallas_call(
        functools.partial(hop_kernel, cols, step, lag, units, (*arrives, n_col), leaves),
        in_specs=[SMEM, ANY, VMEM, VMEM] + [ANY] * (len(own_a) + len(own_b)),
        out_specs=[VMEM, VMEM, ANY],
        out_shape=[out, out, jax.ShapeDtypeStruct(tok.shape, tok.dtype)],
        scratch_shapes=[
            pltpu.VMEM((rows, 2 * units), jnp.bfloat16),
            pltpu.VMEM((rows, 2 * units), jnp.bfloat16),
            pltpu.SemaphoreType.DMA((2,)),
        ],
        input_output_aliases={1: 2},
        compiler_params=pltpu.CompilerParams(vmem_limit_bytes=8 * MIB),
    )(z, tok, left_in, right_in, *[x for _, x in own_a], *[x for _, x in own_b])


def project_kernel(picks, edge, units, z_ref, mask, tok, w, *rest):
    hidden, (out, tok_out, held, acc, sem) = rest[:len(picks)], rest[len(picks):]
    k, steps = pl.program_id(0), pl.num_programs(0)
    z = z_ref[0]

    @pl.when(k == 0)
    def _():
        def each(act):
            for ref, (i, slot, at) in zip(hidden, picks):
                @pl.when(z == i)
                def _(ref=ref, slot=slot, at=at):
                    act(pltpu.make_async_copy(ref.at[:, at:at + units], held.at[slot], sem.at[slot]))
        each(lambda c: c.start())
        acc[...] = jnp.zeros_like(acc)
        each(lambda c: c.wait())

    acc[...] += jnp.dot(
        held[k], masked(w, mask, k * (units // edge), 0, edge), preferred_element_type=jnp.float32
    )

    @pl.when(k == steps - 1)
    def _():
        out[...] = acc[...].astype(out.dtype)


def project(tok, z, hidden, down, mask, units):
    rows = hidden[0][3].shape[0]
    depth, width = down.shape
    edge = depth // mask.shape[0]
    slots = depth // units
    return pl.pallas_call(
        functools.partial(project_kernel, tuple(h[:3] for h in hidden), edge, units),
        grid=(slots,),
        in_specs=[SMEM, SMEM, ANY, pl.BlockSpec((units, width), lambda k: (k, 0))] + [ANY] * len(hidden),
        out_specs=[pl.BlockSpec((rows, width), lambda k: (0, 0)), ANY],
        out_shape=[jax.ShapeDtypeStruct((rows, width), jnp.bfloat16), jax.ShapeDtypeStruct(tok.shape, tok.dtype)],
        scratch_shapes=[
            pltpu.VMEM((slots, rows, units), jnp.bfloat16),
            pltpu.VMEM((rows, width), jnp.float32),
            pltpu.SemaphoreType.DMA((slots,)),
        ],
        input_output_aliases={2: 1},
        compiler_params=pltpu.CompilerParams(vmem_limit_bytes=52 * MIB),
    )(z, mask, tok, down, *[h[3] for h in hidden])


def cycle(n_row, n_col):
    def at(r, i):
        return r * n_col + (n_col - 1 - i if r % 2 else i)

    steps = []
    for r in range(n_row):
        mate = r ^ 1 if r ^ 1 < n_row else r
        steps += [(at(r, i), at(r, i + 1)) for i in range(n_col - 1)] + [(at(r, n_col - 1), at(mate, 0))]
    return steps


def shards(n_row, n_col, tokens, gate, up, down, gm, um, dm):
    lag = LAG
    half = gate.shape[1] // 2
    units = min(512, half)
    n_unit = half // units
    xor = n_row & (n_row - 1) == 0
    other = (lambda i, d: i ^ d) if xor else (lambda i, d: (i + d) % n_row)
    order = [0, *range(2, n_row), 1][:n_row]
    n = n_row * n_unit
    z, odd = lax.axis_index("col"), lax.axis_index("row") % 2
    z = jnp.where(odd == 1, n_col - 1 - z, z).astype(jnp.int32).reshape(1)
    to_right = cycle(n_row, n_col)
    to_left = [(j, i) for i, j in to_right]
    tok = jnp.zeros((8, 128), jnp.float32)

    xs = {0: tokens}
    for d in order[1:]:
        xs[d] = lax.ppermute(tokens, "row", [(other(i, d), i) for i in range(n_row)])

    own_a, own_b = [], []
    left_sent, right_sent, left_got, right_got, kind = {}, {}, {}, {}, {}
    outs = {}
    last_sum = n - 1 + lag * (n_col - 2)
    last_end = n - 1 + lag * (n_col - 1)
    last_hop = n - 1 + lag * (2 * n_col - 3)
    first_end = lag * (n_col - 1)

    def place(k):
        t0 = k + first_end
        spots = []
        for i in range(n_col):
            t = t0 + lag * (i - 1)
            buf, what = (right_sent[t0], kind[t0]) if i == 0 else (right_got[t], kind[t])
            spots.append((i, 0, 2 * units if what[0] else 0, buf))
            j = n_col - 1 - i
            buf, what = (left_sent[t0], kind[t0]) if i == 0 else (left_got[t], kind[t])
            spots.append((j, 1, 2 * units if what[0] else 0, buf))
        return spots

    for t in range(last_hop + lag + 1):
        if t < n:
            pa, pb, tok = partials(tok, xs[order[t // n_unit]], gate, up, gm, um, t % n_unit, units)
            own_a.append(pa)
            own_b.append(pb)
        if t <= last_hop:
            kind[t] = (t <= last_sum, t >= first_end)
            if t < lag:
                left_sent[t], right_sent[t] = own_a[t], own_b[t]
            elif t <= last_end:
                mine_a = [(i, own_a[t - lag * (n_col - 1 - i)]) for i in range(n_col) if 0 <= t - lag * (n_col - 1 - i) < n]
                mine_b = [(i, own_b[t - lag * i]) for i in range(n_col) if 0 <= t - lag * i < n]
                left_sent[t], right_sent[t], tok = hop(
                    tok, z, left_got[t - lag], right_got[t - lag], mine_a, mine_b, t, lag, units, kind[t - lag], kind[t], n_col
                )
            else:
                left_sent[t], right_sent[t] = left_got[t - lag], right_got[t - lag]
                if kind[t - lag][0]:
                    left_sent[t], right_sent[t] = left_sent[t][:, 2 * units:], right_sent[t][:, 2 * units:]
            left_got[t] = lax.ppermute(left_sent[t], ("row", "col"), to_left)
            right_got[t] = lax.ppermute(right_sent[t], ("row", "col"), to_right)
        done = t - lag * (2 * n_col - 2)
        if done >= 0 and done % n_unit == n_unit - 1:
            b = done // n_unit
            hidden = []
            for u in range(n_unit):
                for i, side, at, buf in place(b * n_unit + u):
                    hidden.append((i, side * n_unit + u, at, buf))
            outs[order[b]], tok = project(tok, z, hidden, down, dm, units)

    total = outs[0].astype(jnp.float32)
    for d in order[1:]:
        total = total + lax.ppermute(
            outs[d], "row", [(i, other(i, d)) for i in range(n_row)]
        ).astype(jnp.float32)
    return total.astype(jnp.bfloat16)


def solution(mesh):
    in_specs = (
        P(("groups", "row"), "col"),
        P("col", "row"),
        P("col", "row"),
        P("row", "col"),
        P("col", "row"),
        P("col", "row"),
        P("row", "col"),
    )
    out_specs = P(("groups", "row"), "col")
    body = functools.partial(shards, mesh.shape["row"], mesh.shape["col"])
    return jax.shard_map(body, mesh=mesh, in_specs=in_specs, out_specs=out_specs, check_vma=False)
```

time: 422 us -> 231 us (0.55)
  waiting for transfers between devices: 259 us -> 20.1 us
  Pallas kernels: 0 us -> 136 us
  local copies, waits for them, and re-layouts: 75.1 us -> 8.81 us
  starting transfers between devices: 0.3 us -> 62.3 us
  matrix products: 41.2 us -> 0 us
  other arithmetic: 33 us -> 1.13 us
  between operations: 13.2 us -> 1.63 us
    unnamed x5 -> x0, waiting for transfers between devices: 148 us -> none
    pallas_call x0 -> x40, Pallas kernels: none -> 136 us  [the longest x16 80.2 us: partials(): pl.pallas_call(functools.partial(partial_kernel, edge, (unit * units // e...]
    all_gather x2 -> x0, waiting for transfers between devices: 81.1 us -> none  [the longest x1 81.1 us: shards(): lax.all_gather(hidden, 'col', axis=0, tiled=True)]
    ppermute x0 -> x58, starting transfers between devices: none -> 62.3 us  [the longest x26 45.1 us: shards(): right_got[t] = lax.ppermute(right_sent[t], ('row', 'col'), to_right)]
    broadcast_in_dim x6 -> x1, local copies, waits for them, and re-layouts: 60.4 us -> 0.01 us  [shards(): tok = jnp.zeros((8, 128), jnp.float32)]
    dot_general x2 -> x0, matrix products: 41.2 us -> none  [the longest x1 24.9 us: shards(): jnp.dot(lax.all_gather(tokens, 'row', axis=0, tiled=True), both_pruned, p...]
    mul x1 -> x0, other arithmetic: 29.8 us -> none  [pruned(): return weight * spread.astype(jnp.bfloat16)]
    reduce_scatter x1 -> x0, waiting for transfers between devices: 29.8 us -> none  [shards(): lax.psum_scatter(terms.astype(jnp.bfloat16), 'row', scatter_dimension=0,...]
  transfers between devices with their start and end apart: 4 -> 58, of which waited for: 3 -> 16; matrix products, arithmetic and copies ran while one was open for 17% -> 0% of each run, Pallas kernels for 0% -> 57%
where the time goes in v1:
time: 231 us; the launch traced here: 230 us
  Pallas kernels  136 us (59%)
  starting transfers between devices  62.3 us (27%)
  waiting for transfers between devices  20.1 us (9%)
  local copies, waits for them, and re-layouts  8.81 us (4%)
    pallas_call x16, Pallas kernels, partials(): pl.pallas_call(functools.partial(partial_kernel, edge, (unit * units // e...  80.2 us
    pallas_call x4, Pallas kernels, project(): pl.pallas_call(functools.partial(project_kernel, tuple((h[:3] for h in hi...  47.4 us
    ppermute x26, starting transfers between devices, shards(): right_got[t] = lax.ppermute(right_sent[t], ('row', 'col'), to_right)  45.1 us
    ppermute x26, starting transfers between devices, shards(): left_got[t] = lax.ppermute(left_sent[t], ('row', 'col'), to_left)  13.5 us
    ppermute x26, waiting for transfers between devices, shards(): left_got[t] = lax.ppermute(left_sent[t], ('row', 'col'), to_left)  12.6 us
    unnamed x175, local copies, waits for them, and re-layouts  8.81 us
    pallas_call x20, Pallas kernels, hop(): pl.pallas_call(functools.partial(hop_kernel, cols, step, lag, units, (*ar...  8.15 us
    ppermute x26, waiting for transfers between devices, shards(): right_got[t] = lax.ppermute(right_sent[t], ('row', 'col'), to_right)  5.72 us
  transfers between devices with their start and end apart: 58, of which 16 were waited for; matrix products, arithmetic and copies ran while one was open for 0% of the time, Pallas kernels for 57%

profile of v1, /device:TPU:0, one launch (start us, length us, event | category | flops | bytes accessed | tf_op | source)
XLA Modules:
  0.0 229.7 jit_solution(16040878524230338358)
XLA Ops:
  1.4 5.1 %shard_map.73 = (bf16[128,1024]{1,0:T(8,128)(2,1)S(1)}, bf16[128,1024]{1,0:T(8,128)(2,1)S(1)}, f32[8,128]{1,0:T(8,128)S(1)}) custom-call(s32[16,32]{1,0:T(8,128)S(1)} %copy-done.45, s32[16,32]{1,0:T(8,128)S(1)} %copy-done.47, f32[8,128]{1,0:T(8,128)S(1)} %broadcast_in_dim.3.tok, bf16[128,2048]{1,0:T(8,128)(2,1)} %x.7, ...), custom_call_target="tpu_custom_call", output_to_operand_aliasing={{2}: (2, {})} | custom-call | tf_op jit(solution)/shard_map/pallas_call | solution.py:56
  7.0 2.6 %collective-permute-start.1 = (bf16[128,1024]{1,0:T(8,128)(2,1)S(1)}, bf16[128,1024]{1,0:T(8,128)(2,1)S(1)}, u32[]{:S(2)}, u32[]{:S(2)}) collective-permute-start(bf16[128,1024]{1,0:T(8,128)(2,1)S(1)} %get-tuple-element.124.rest_3_.rest_5_.rest_7_), channel_id=1, source_target_pairs={{0,1},{1,2},{2,3},{3,7},{7,6},{6,5},{5,4},{4,0},{8,9},{9,10},{10,1... | collective-permute-start | bytes 786440 | tf_op jit(solution)/shard_map/ppermute | solution.py:269
  11.5 5.1 %shard_map.74 = (bf16[128,1024]{1,0:T(8,128)(2,1)S(1)}, bf16[128,1024]{1,0:T(8,128)(2,1)S(1)}, f32[8,128]{1,0:T(8,128)S(1)}) custom-call(s32[16,32]{1,0:T(8,128)S(1)} %copy-done.45, s32[16,32]{1,0:T(8,128)S(1)} %copy-done.47, f32[8,128]{1,0:T(8,128)S(1)} %get-tuple-element.120.tok, bf16[128,2048]{1,0:T(8,128)(2,1)} %x.7, ...), custom_call_target="tpu_custom_call", output_to_operand_aliasing={{2}: (2, {})} | custom-call | tf_op jit(solution)/shard_map/pallas_call | solution.py:56
  16.7 2.0 collective-permute-start.3
  18.7 5.1 %shard_map.75 = (bf16[128,1024]{1,0:T(8,128)(2,1)S(1)}, bf16[128,1024]{1,0:T(8,128)(2,1)S(1)}, f32[8,128]{1,0:T(8,128)S(1)}) custom-call(s32[16,32]{1,0:T(8,128)S(1)} %copy-done.46, s32[16,32]{1,0:T(8,128)S(1)} %copy-done.48, f32[8,128]{1,0:T(8,128)S(1)} %get-tuple-element.121.tok, bf16[128,2048]{1,0:T(8,128)(2,1)} %x.7, ...), custom_call_target="tpu_custom_call", output_to_operand_aliasing={{2}: (2, {})} | custom-call | tf_op jit(solution)/shard_map/pallas_call | solution.py:56
  26.0 5.1 %shard_map.77 = (bf16[128,1024]{1,0:T(8,128)(2,1)S(1)}, bf16[128,1024]{1,0:T(8,128)(2,1)S(1)}, f32[8,128]{1,0:T(8,128)S(1)}) custom-call(s32[16,32]{1,0:T(8,128)S(1)} %copy-done.46, s32[16,32]{1,0:T(8,128)S(1)} %copy-done.48, f32[8,128]{1,0:T(8,128)S(1)} %get-tuple-element.127.tok, bf16[128,2048]{1,0:T(8,128)(2,1)} %x.7, ...), custom_call_target="tpu_custom_call", output_to_operand_aliasing={{2}: (2, {})} | custom-call | tf_op jit(solution)/shard_map/pallas_call | solution.py:56
  33.2 5.0 %shard_map.79 = (bf16[128,1024]{1,0:T(8,128)(2,1)S(1)}, bf16[128,1024]{1,0:T(8,128)(2,1)S(1)}, f32[8,128]{1,0:T(8,128)S(1)}) custom-call(s32[16,32]{1,0:T(8,128)S(1)} %copy-done.46, s32[16,32]{1,0:T(8,128)S(1)} %copy-done.48, f32[8,128]{1,0:T(8,128)S(1)} %get-tuple-element.133.tok, ...), custom_call_target="tpu_custom_call", output_to_operand_aliasing={{2}: (2, {})} | custom-call | tf_op jit(solution)/shard_map/pallas_call | solution.py:56
  38.4 2.2 collective-permute-start.10
  40.5 5.0 %shard_map.81 = (bf16[128,1024]{1,0:T(8,128)(2,1)S(1)}, bf16[128,1024]{1,0:T(8,128)(2,1)S(1)}, f32[8,128]{1,0:T(8,128)S(1)}) custom-call(s32[16,32]{1,0:T(8,128)S(1)} %copy-done.46, s32[16,32]{1,0:T(8,128)S(1)} %copy-done.48, f32[8,128]{1,0:T(8,128)S(1)} %get-tuple-element.139.tok, ...), custom_call_target="tpu_custom_call", output_to_operand_aliasing={{2}: (2, {})} | custom-call | tf_op jit(solution)/shard_map/pallas_call | solution.py:56
  45.7 2.2 collective-permute-start.12
  47.9 5.0 %shard_map.83 = (bf16[128,1024]{1,0:T(8,128)(2,1)S(1)}, bf16[128,1024]{1,0:T(8,128)(2,1)S(1)}, f32[8,128]{1,0:T(8,128)S(1)}) custom-call(s32[16,32]{1,0:T(8,128)S(1)} %copy-done.46, s32[16,32]{1,0:T(8,128)S(1)} %copy-done.48, f32[8,128]{1,0:T(8,128)S(1)} %get-tuple-element.145.tok, ...), custom_call_target="tpu_custom_call", output_to_operand_aliasing={{2}: (2, {})} | custom-call | tf_op jit(solution)/shard_map/pallas_call | solution.py:56
  55.4 5.0 %shard_map.85 = (bf16[128,1024]{1,0:T(8,128)(2,1)S(1)}, bf16[128,1024]{1,0:T(8,128)(2,1)S(1)}, f32[8,128]{1,0:T(8,128)S(1)}) custom-call(s32[16,32]{1,0:T(8,128)S(1)} %copy-done.46, s32[16,32]{1,0:T(8,128)S(1)} %copy-done.48, f32[8,128]{1,0:T(8,128)S(1)} %get-tuple-element.151.tok, ...), custom_call_target="tpu_custom_call", output_to_operand_aliasing={{2}: (2, {})} | custom-call | tf_op jit(solution)/shard_map/pallas_call | solution.py:56
  62.9 5.0 %shard_map.87 = (bf16[128,1024]{1,0:T(8,128)(2,1)S(1)}, bf16[128,1024]{1,0:T(8,128)(2,1)S(1)}, f32[8,128]{1,0:T(8,128)S(1)}) custom-call(s32[16,32]{1,0:T(8,128)S(1)} %copy-done.46, s32[16,32]{1,0:T(8,128)S(1)} %copy-done.48, f32[8,128]{1,0:T(8,128)S(1)} %get-tuple-element.157.tok, ...), custom_call_target="tpu_custom_call", output_to_operand_aliasing={{2}: (2, {})} | custom-call | tf_op jit(solution)/shard_map/pallas_call | solution.py:56
  70.4 5.0 %shard_map.89 = (bf16[128,1024]{1,0:T(8,128)(2,1)S(1)}, bf16[128,1024]{1,0:T(8,128)(2,1)S(1)}, f32[8,128]{1,0:T(8,128)S(1)}) custom-call(s32[16,32]{1,0:T(8,128)S(1)} %copy-done.46, s32[16,32]{1,0:T(8,128)S(1)} %copy-done.48, f32[8,128]{1,0:T(8,128)S(1)} %get-tuple-element.163.tok, ...), custom_call_target="tpu_custom_call", output_to_operand_aliasing={{2}: (2, {})} | custom-call | tf_op jit(solution)/shard_map/pallas_call | solution.py:56
  78.0 5.0 %shard_map.91 = (bf16[128,1024]{1,0:T(8,128)(2,1)S(1)}, bf16[128,1024]{1,0:T(8,128)(2,1)S(1)}, f32[8,128]{1,0:T(8,128)S(1)}) custom-call(s32[16,32]{1,0:T(8,128)S(1)} %copy-done.46, s32[16,32]{1,0:T(8,128)S(1)} %copy-done.48, f32[8,128]{1,0:T(8,128)S(1)} %get-tuple-element.169.tok, ...), custom_call_target="tpu_custom_call", output_to_operand_aliasing={{2}: (2, {})} | custom-call | tf_op jit(solution)/shard_map/pallas_call | solution.py:56
  85.5 5.0 %shard_map.93 = (bf16[128,1024]{1,0:T(8,128)(2,1)S(1)}, bf16[128,1024]{1,0:T(8,128)(2,1)S(1)}, f32[8,128]{1,0:T(8,128)S(1)}) custom-call(s32[16,32]{1,0:T(8,128)S(1)} %copy-done.46, s32[16,32]{1,0:T(8,128)S(1)} %copy-done.48, f32[8,128]{1,0:T(8,128)S(1)} %get-tuple-element.175.tok, ...), custom_call_target="tpu_custom_call", output_to_operand_aliasing={{2}: (2, {})} | custom-call | tf_op jit(solution)/shard_map/pallas_call | solution.py:56
  93.3 5.0 %shard_map.95 = (bf16[128,1024]{1,0:T(8,128)(2,1)S(1)}, bf16[128,1024]{1,0:T(8,128)(2,1)S(1)}, f32[8,128]{1,0:T(8,128)S(1)}) custom-call(s32[16,32]{1,0:T(8,128)S(1)} %copy-done.46, s32[16,32]{1,0:T(8,128)S(1)} %copy-done.48, f32[8,128]{1,0:T(8,128)S(1)} %get-tuple-element.181.tok, ...), custom_call_target="tpu_custom_call", output_to_operand_aliasing={{2}: (2, {})} | custom-call | tf_op jit(solution)/shard_map/pallas_call | solution.py:56
  101.6 5.0 %shard_map.97 = (bf16[128,1024]{1,0:T(8,128)(2,1)S(1)}, bf16[128,1024]{1,0:T(8,128)(2,1)S(1)}, f32[8,128]{1,0:T(8,128)S(1)}) custom-call(s32[16,32]{1,0:T(8,128)S(1)} %copy-done.46, s32[16,32]{1,0:T(8,128)S(1)} %copy-done.49, f32[8,128]{1,0:T(8,128)S(1)} %get-tuple-element.187.tok, ...), custom_call_target="tpu_custom_call", output_to_operand_aliasing={{2}: (2, {})} | custom-call | tf_op jit(solution)/shard_map/pallas_call | solution.py:56
  109.8 5.0 %shard_map.99 = (bf16[128,1024]{1,0:T(8,128)(2,1)S(1)}, bf16[128,1024]{1,0:T(8,128)(2,1)S(1)}, f32[8,128]{1,0:T(8,128)S(1)}) custom-call(s32[16,32]{1,0:T(8,128)S(1)} %copy-done.46, s32[16,32]{1,0:T(8,128)S(1)} %copy-done.49, f32[8,128]{1,0:T(8,128)S(1)} %get-tuple-element.193.tok, ...), custom_call_target="tpu_custom_call", output_to_operand_aliasing={{2}: (2, {})} | custom-call | tf_op jit(solution)/shard_map/pallas_call | solution.py:56
  119.1 5.0 %shard_map.101 = (bf16[128,1024]{1,0:T(8,128)(2,1)S(1)}, bf16[128,1024]{1,0:T(8,128)(2,1)S(1)}, f32[8,128]{1,0:T(8,128)S(1)}) custom-call(s32[16,32]{1,0:T(8,128)S(1)} %copy-done.46, s32[16,32]{1,0:T(8,128)S(1)} %copy-done.49, f32[8,128]{1,0:T(8,128)S(1)} %get-tuple-element.199.tok, ...), custom_call_target="tpu_custom_call", output_to_operand_aliasing={{2}: (2, {})} | custom-call | tf_op jit(solution)/shard_map/pallas_call | solution.py:56
  132.9 11.8 %shard_map.103 = (bf16[128,2048]{1,0:T(8,128)(2,1)}, f32[8,128]{1,0:T(8,128)S(1)}) custom-call(s32[1]{0:T(128)} %bitcast.z_ref, s32[32,16]{1,0:T(8,128)S(1)} %copy.48.mask, f32[8,128]{1,0:T(8,128)S(1)} %get-tuple-element.205.tok, bf16[4096,2048]{1,0:T(8,128)(2,1)} %w.7, bf16[128,1536]{1,0:T(8,128)(2,1)S(1)} %copy-done.59, ...), custom_call_target="tpu_custom_call", output_to_operand_aliasing={{1}: (2, {})} | custom-call | tf_op jit(solution)/shard_map/pallas_call | solution.py:183
  149.7 6.2 %collective-permute-done.35.left_in.rest_23_.rest_5_.rest_19_ = bf16[128,1536]{1,0:T(8,128)(2,1)S(1)} collective-permute-done((bf16[128,1536]{1,0:T(8,128)(2,1)S(1)}, bf16[128,1536]{1,0:T(8,128)(2,1)S(1)}, u32[]{:S(2)}, u32[]{:S(2)}) %collective-permute-start.35) | collective-permute-done | bytes 393248 | tf_op jit(solution)/shard_map/ppermute | solution.py:268
  159.5 4.9 %collective-permute-done.37.left_in.rest_31_.rest_13_.rest_27_ = bf16[128,1536]{1,0:T(8,128)(2,1)S(1)} collective-permute-done((bf16[128,1536]{1,0:T(8,128)(2,1)S(1)}, bf16[128,1536]{1,0:T(8,128)(2,1)S(1)}, u32[]{:S(2)}, u32[]{:S(2)}) %collective-permute-start.37) | collective-permute-done | bytes 393248 | tf_op jit(solution)/shard_map/ppermute | solution.py:268
  168.0 11.7 %shard_map.108 = (bf16[128,2048]{1,0:T(8,128)(2,1)}, f32[8,128]{1,0:T(8,128)S(1)}) custom-call(s32[1]{0:T(128)} %bitcast.z_ref, s32[32,16]{1,0:T(8,128)S(1)} %copy.48.mask, f32[8,128]{1,0:T(8,128)S(1)} %get-tuple-element.219.tok, bf16[4096,2048]{1,0:T(8,128)(2,1)} %w.7, bf16[128,1536]{1,0:T(8,128)(2,1)S(1)} %copy-done.63, ...), custom_call_target="tpu_custom_call", output_to_operand_aliasing={{1}: (2, {})} | custom-call | tf_op jit(solution)/shard_map/pallas_call | solution.py:183
  181.8 2.3 collective-permute-start.46
  184.1 2.0 collective-permute-start.44
  187.9 2.5 %collective-permute-start.51 = (bf16[128,512]{1,0:T(8,128)(2,1)S(1)}, bf16[128,512]{1,0:T(8,128)(2,1)S(1)}, u32[]{:S(2)}, u32[]{:S(2)}) collective-permute-start(bf16[128,512]{1,0:T(8,128)(2,1)S(1)} %collective-permute-done.46.rest_30_.rest_12_.rest_26_), channel_id=1, source_target_pairs={{0,1},{1,2},{2,3},{3,7},{7,6},{6,5},{5,4},{4,0},{8,9},{9,10},{10,1... | collective-permute-start | bytes 393224 | tf_op jit(solution)/shard_map/ppermute | solution.py:269
  190.7 2.5 %collective-permute-start.49 = (bf16[128,512]{1,0:T(8,128)(2,1)S(1)}, bf16[128,512]{1,0:T(8,128)(2,1)S(1)}, u32[]{:S(2)}, u32[]{:S(2)}) collective-permute-start(bf16[128,512]{1,0:T(8,128)(2,1)S(1)} %collective-permute-done.44.rest_22_.rest_4_.rest_18_), channel_id=1, source_target_pairs={{0,1},{1,2},{2,3},{3,7},{7,6},{6,5},{5,4},{4,0},{8,9},{9,10},{10,1... | collective-permute-start | bytes 393224 | tf_op jit(solution)/shard_map/ppermute | solution.py:269
  193.7 2.5 %collective-permute-start.55 = (bf16[128,512]{1,0:T(8,128)(2,1)S(1)}, bf16[128,512]{1,0:T(8,128)(2,1)S(1)}, u32[]{:S(2)}, u32[]{:S(2)}) collective-permute-start(bf16[128,512]{1,0:T(8,128)(2,1)S(1)} %collective-permute-done.51.rest_14_.rest_28_), channel_id=1, source_target_pairs={{0,1},{1,2},{2,3},{3,7},{7,6},{6,5},{5,4},{4,0},{8,9},{9,10},{10,1... | collective-permute-start | bytes 393224 | tf_op jit(solution)/shard_map/ppermute | solution.py:269
  196.9 2.5 %collective-permute-start.53 = (bf16[128,512]{1,0:T(8,128)(2,1)S(1)}, bf16[128,512]{1,0:T(8,128)(2,1)S(1)}, u32[]{:S(2)}, u32[]{:S(2)}) collective-permute-start(bf16[128,512]{1,0:T(8,128)(2,1)S(1)} %collective-permute-done.49.rest_6_.rest_20_), channel_id=1, source_target_pairs={{0,1},{1,2},{2,3},{3,7},{7,6},{6,5},{5,4},{4,0},{8,9},{9,10},{10,1... | collective-permute-start | bytes 393224 | tf_op jit(solution)/shard_map/ppermute | solution.py:269
  200.8 11.6 %shard_map.111 = (bf16[128,2048]{1,0:T(8,128)(2,1)}, f32[8,128]{1,0:T(8,128)S(1)}) custom-call(s32[1]{0:T(128)} %bitcast.z_ref, s32[32,16]{1,0:T(8,128)S(1)} %copy.48.mask, f32[8,128]{1,0:T(8,128)S(1)} %get-tuple-element.227.tok, bf16[4096,2048]{1,0:T(8,128)(2,1)} %w.7, ...), custom_call_target="tpu_custom_call", output_to_operand_aliasing={{1}: (2, {})} | custom-call | tf_op jit(solution)/shard_map/pallas_call | solution.py:183
  213.1 12.3 %shard_map.112 = (bf16[128,2048]{1,0:T(8,128)(2,1)}, f32[8,128]{1,0:T(8,128)S(1)}) custom-call(s32[1]{0:T(128)} %bitcast.z_ref, s32[32,16]{1,0:T(8,128)S(1)} %copy.48.mask, f32[8,128]{1,0:T(8,128)S(1)} %get-tuple-element.233.tok, bf16[4096,2048]{1,0:T(8,128)(2,1)} %w.7, bf16[128,1536]{1,0:T(8,128)(2,1)} %copy-done.77, ...), custom_call_target="tpu_custom_call", output_to_operand_aliasing={{1}: (2, {})} | custom-call | tf_op jit(solution)/shard_map/pallas_call | solution.py:183
  (301 shorter events, 66.1 us)
Async XLA Ops:
  6.5 17.3 %collective-permute-start = (bf16[128,1024]{1,0:T(8,128)(2,1)S(1)}, bf16[128,1024]{1,0:T(8,128)(2,1)S(1)}, u32[]{:S(2)}, u32[]{:S(2)}) collective-permute-start(bf16[128,1024]{1,0:T(8,128)(2,1)S(1)} %get-tuple-element.123.rest_0_), channel_id=1, source_target_pairs={{1,0},{2,1},{3,2},{7,3},{6,7},{5,6},{4,5},{0,4},{9,8},{10,9},{11,1... | collective-permute-start | bytes 786440 | tf_op jit(solution)/shard_map/ppermute | solution.py:268
  7.0 16.8 %collective-permute-start.1 = (bf16[128,1024]{1,0:T(8,128)(2,1)S(1)}, bf16[128,1024]{1,0:T(8,128)(2,1)S(1)}, u32[]{:S(2)}, u32[]{:S(2)}) collective-permute-start(bf16[128,1024]{1,0:T(8,128)(2,1)S(1)} %get-tuple-element.124.rest_3_.rest_5_.rest_7_), channel_id=1, source_target_pairs={{0,1},{1,2},{2,3},{3,7},{7,6},{6,5},{5,4},{4,0},{8,9},{9,10},{10,1... | collective-permute-start | bytes 786440 | tf_op jit(solution)/shard_map/ppermute | solution.py:269
  9.6 23.7 %collective-permute-start.4 = (bf16[128,2048]{1,0:T(8,128)(2,1)}, bf16[128,2048]{1,0:T(8,128)(2,1)S(1)}, u32[]{:S(2)}, u32[]{:S(2)}) collective-permute-start(bf16[128,2048]{1,0:T(8,128)(2,1)} %x.7), channel_id=1, source_target_pairs={{8,0},{12,4},{0,8},{4,12},{9,1},{13,5},{1,9},{5,13},{10,2},{14,6},... | collective-permute-start | bytes 1572872 | tf_op jit(solution)/shard_map/ppermute | solution.py:227
  38.4 14.6 %collective-permute-start.9 = (bf16[128,1024]{1,0:T(8,128)(2,1)S(1)}, bf16[128,1024]{1,0:T(8,128)(2,1)S(1)}, u32[]{:S(2)}, u32[]{:S(2)}) collective-permute-start(bf16[128,1024]{1,0:T(8,128)(2,1)S(1)} %get-tuple-element.147), channel_id=1, source_target_pairs={{1,0},{2,1},{3,2},{7,3},{6,7},{5,6},{4,5},{0,4},{9,8},{10,9},{11,1... | collective-permute-start | bytes 786440 | tf_op jit(solution)/shard_map/ppermute | solution.py:268
  45.7 14.7 %collective-permute-start.11 = (bf16[128,1024]{1,0:T(8,128)(2,1)S(1)}, bf16[128,1024]{1,0:T(8,128)(2,1)S(1)}, u32[]{:S(2)}, u32[]{:S(2)}) collective-permute-start(bf16[128,1024]{1,0:T(8,128)(2,1)S(1)} %get-tuple-element.153), channel_id=1, source_target_pairs={{1,0},{2,1},{3,2},{7,3},{6,7},{5,6},{4,5},{0,4},{9,8},{10,9},{11,1... | collective-permute-start | bytes 786440 | tf_op jit(solution)/shard_map/ppermute | solution.py:268
  45.7 14.7 %collective-permute-start.12 = (bf16[128,1024]{1,0:T(8,128)(2,1)S(1)}, bf16[128,1024]{1,0:T(8,128)(2,1)S(1)}, u32[]{:S(2)}, u32[]{:S(2)}) collective-permute-start(bf16[128,1024]{1,0:T(8,128)(2,1)S(1)} %get-tuple-element.154), channel_id=1, source_target_pairs={{0,1},{1,2},{2,3},{3,7},{7,6},{6,5},{5,4},{4,0},{8,9},{9,10},{10,1... | collective-permute-start | bytes 786440 | tf_op jit(solution)/shard_map/ppermute | solution.py:269
  47.9 14.9 %collective-permute-start.13 = (bf16[128,2048]{1,0:T(8,128)(2,1)}, bf16[128,2048]{1,0:T(8,128)(2,1)S(1)}, u32[]{:S(2)}, u32[]{:S(2)}) collective-permute-start(bf16[128,2048]{1,0:T(8,128)(2,1)} %x.7), channel_id=1, source_target_pairs={{12,0},{8,4},{4,8},{0,12},{13,1},{9,5},{5,9},{1,13},{14,2},{10,6},... | collective-permute-start | bytes 1572872 | tf_op jit(solution)/shard_map/ppermute | solution.py:227
  60.8 14.6 %collective-permute-start.16 = (bf16[128,1536]{1,0:T(8,128)(2,1)S(1)}, bf16[128,1536]{1,0:T(8,128)(2,1)S(1)}, u32[]{:S(2)}, u32[]{:S(2)}) collective-permute-start(bf16[128,1536]{1,0:T(8,128)(2,1)S(1)} %get-tuple-element.165.rest_9_), channel_id=1, source_target_pairs={{1,0},{2,1},{3,2},{7,3},{6,7},{5,6},{4,5},{0,4},{9,8},{10,9},{11,1... | collective-permute-start | bytes 1179656 | tf_op jit(solution)/shard_map/ppermute | solution.py:268
  68.3 14.7 %collective-permute-start.18 = (bf16[128,1536]{1,0:T(8,128)(2,1)S(1)}, bf16[128,1536]{1,0:T(8,128)(2,1)S(1)}, u32[]{:S(2)}, u32[]{:S(2)}) collective-permute-start(bf16[128,1536]{1,0:T(8,128)(2,1)S(1)} %get-tuple-element.171.rest_17_), channel_id=1, source_target_pairs={{1,0},{2,1},{3,2},{7,3},{6,7},{5,6},{4,5},{0,4},{9,8},{10,9},{11,1... | collective-permute-start | bytes 1179656 | tf_op jit(solution)/shard_map/ppermute | solution.py:268
  68.3 14.7 %collective-permute-start.19 = (bf16[128,1536]{1,0:T(8,128)(2,1)S(1)}, bf16[128,1536]{1,0:T(8,128)(2,1)S(1)}, u32[]{:S(2)}, u32[]{:S(2)}) collective-permute-start(bf16[128,1536]{1,0:T(8,128)(2,1)S(1)} %get-tuple-element.172.rest_16_), channel_id=1, source_target_pairs={{0,1},{1,2},{2,3},{3,7},{7,6},{6,5},{5,4},{4,0},{8,9},{9,10},{10,1... | collective-permute-start | bytes 1179656 | tf_op jit(solution)/shard_map/ppermute | solution.py:269
  75.8 14.7 %collective-permute-start.20 = (bf16[128,1536]{1,0:T(8,128)(2,1)S(1)}, bf16[128,1536]{1,0:T(8,128)(2,1)S(1)}, u32[]{:S(2)}, u32[]{:S(2)}) collective-permute-start(bf16[128,1536]{1,0:T(8,128)(2,1)S(1)} %get-tuple-element.177.rest_25_), channel_id=1, source_target_pairs={{1,0},{2,1},{3,2},{7,3},{6,7},{5,6},{4,5},{0,4},{9,8},{10,9},{11,1... | collective-permute-start | bytes 1179656 | tf_op jit(solution)/shard_map/ppermute | solution.py:268
  78.0 15.3 %collective-permute-start.22 = (bf16[128,2048]{1,0:T(8,128)(2,1)}, bf16[128,2048]{1,0:T(8,128)(2,1)S(1)}, u32[]{:S(2)}, u32[]{:S(2)}) collective-permute-start(bf16[128,2048]{1,0:T(8,128)(2,1)} %x.7), channel_id=1, source_target_pairs={{4,0},{0,4},{12,8},{8,12},{5,1},{1,5},{13,9},{9,13},{6,2},{2,6},{1... | collective-permute-start | bytes 1572872 | tf_op jit(solution)/shard_map/ppermute | solution.py:227
  83.5 14.9 %collective-permute-start.23 = (bf16[128,1536]{1,0:T(8,128)(2,1)S(1)}, bf16[128,1536]{1,0:T(8,128)(2,1)S(1)}, u32[]{:S(2)}, u32[]{:S(2)}) collective-permute-start(bf16[128,1536]{1,0:T(8,128)(2,1)S(1)} %get-tuple-element.183.rest_1_), channel_id=1, source_target_pairs={{1,0},{2,1},{3,2},{7,3},{6,7},{5,6},{4,5},{0,4},{9,8},{10,9},{11,1... | collective-permute-start | bytes 1179656 | tf_op jit(solution)/shard_map/ppermute | solution.py:268
  91.0 15.6 %collective-permute-start.25 = (bf16[128,1536]{1,0:T(8,128)(2,1)S(1)}, bf16[128,1536]{1,0:T(8,128)(2,1)S(1)}, u32[]{:S(2)}, u32[]{:S(2)}) collective-permute-start(bf16[128,1536]{1,0:T(8,128)(2,1)S(1)} %get-tuple-element.189.rest_9_), channel_id=1, source_target_pairs={{1,0},{2,1},{3,2},{7,3},{6,7},{5,6},{4,5},{0,4},{9,8},{10,9},{11,1... | collective-permute-start | bytes 1179656 | tf_op jit(solution)/shard_map/ppermute | solution.py:268
  92.0 14.9 %collective-permute-start.26 = (bf16[128,1536]{1,0:T(8,128)(2,1)S(1)}, bf16[128,1536]{1,0:T(8,128)(2,1)S(1)}, u32[]{:S(2)}, u32[]{:S(2)}) collective-permute-start(bf16[128,1536]{1,0:T(8,128)(2,1)S(1)} %get-tuple-element.190.rest_8_), channel_id=1, source_target_pairs={{0,1},{1,2},{2,3},{3,7},{7,6},{6,5},{5,4},{4,0},{8,9},{9,10},{10,1... | collective-permute-start | bytes 1179656 | tf_op jit(solution)/shard_map/ppermute | solution.py:269
  99.1 15.9 %collective-permute-start.27 = (bf16[128,1536]{1,0:T(8,128)(2,1)S(1)}, bf16[128,1536]{1,0:T(8,128)(2,1)S(1)}, u32[]{:S(2)}, u32[]{:S(2)}) collective-permute-start(bf16[128,1536]{1,0:T(8,128)(2,1)S(1)} %get-tuple-element.195.rest_17_), channel_id=1, source_target_pairs={{1,0},{2,1},{3,2},{7,3},{6,7},{5,6},{4,5},{0,4},{9,8},{10,9},{11,1... | collective-permute-start | bytes 1179656 | tf_op jit(solution)/shard_map/ppermute | solution.py:268
  100.6 14.7 %collective-permute-start.28 = (bf16[128,1536]{1,0:T(8,128)(2,1)S(1)}, bf16[128,1536]{1,0:T(8,128)(2,1)S(1)}, u32[]{:S(2)}, u32[]{:S(2)}) collective-permute-start(bf16[128,1536]{1,0:T(8,128)(2,1)S(1)} %get-tuple-element.196.rest_16_), channel_id=1, source_target_pairs={{0,1},{1,2},{2,3},{3,7},{7,6},{6,5},{5,4},{4,0},{8,9},{9,10},{10,1... | collective-permute-start | bytes 1179656 | tf_op jit(solution)/shard_map/ppermute | solution.py:269
  107.3 16.8 %collective-permute-start.29 = (bf16[128,1536]{1,0:T(8,128)(2,1)S(1)}, bf16[128,1536]{1,0:T(8,128)(2,1)S(1)}, u32[]{:S(2)}, u32[]{:S(2)}) collective-permute-start(bf16[128,1536]{1,0:T(8,128)(2,1)S(1)} %get-tuple-element.201.rest_25_), channel_id=1, source_target_pairs={{1,0},{2,1},{3,2},{7,3},{6,7},{5,6},{4,5},{0,4},{9,8},{10,9},{11,1... | collective-permute-start | bytes 1179656 | tf_op jit(solution)/shard_map/ppermute | solution.py:268
  108.9 15.3 %collective-permute-start.30 = (bf16[128,1536]{1,0:T(8,128)(2,1)S(1)}, bf16[128,1536]{1,0:T(8,128)(2,1)S(1)}, u32[]{:S(2)}, u32[]{:S(2)}) collective-permute-start(bf16[128,1536]{1,0:T(8,128)(2,1)S(1)} %get-tuple-element.202.rest_24_), channel_id=1, source_target_pairs={{0,1},{1,2},{2,3},{3,7},{7,6},{6,5},{5,4},{4,0},{8,9},{9,10},{10,1... | collective-permute-start | bytes 1179656 | tf_op jit(solution)/shard_map/ppermute | solution.py:269
  116.6 28.1 %collective-permute-start.31 = (bf16[128,1536]{1,0:T(8,128)(2,1)}, bf16[128,1536]{1,0:T(8,128)(2,1)S(1)}, u32[]{:S(2)}, u32[]{:S(2)}) collective-permute-start(bf16[128,1536]{1,0:T(8,128)(2,1)} %get-tuple-element.208.rest_1_), channel_id=1, source_target_pairs={{1,0},{2,1},{3,2},{7,3},{6,7},{5,6},{4,5},{0,4},{9,8},{10,9},{11,1... | collective-permute-start | bytes 1179656 | tf_op jit(solution)/shard_map/ppermute | solution.py:268
  118.2 26.5 %collective-permute-start.32 = (bf16[128,1536]{1,0:T(8,128)(2,1)}, bf16[128,1536]{1,0:T(8,128)(2,1)S(1)}, u32[]{:S(2)}, u32[]{:S(2)}) collective-permute-start(bf16[128,1536]{1,0:T(8,128)(2,1)} %get-tuple-element.209.rest_0_), channel_id=1, source_target_pairs={{0,1},{1,2},{2,3},{3,7},{7,6},{6,5},{5,4},{4,0},{8,9},{9,10},{10,1... | collective-permute-start | bytes 1179656 | tf_op jit(solution)/shard_map/ppermute | solution.py:269
  125.5 21.7 %collective-permute-start.33 = (bf16[128,1536]{1,0:T(8,128)(2,1)}, bf16[128,1536]{1,0:T(8,128)(2,1)S(1)}, u32[]{:S(2)}, u32[]{:S(2)}) collective-permute-start(bf16[128,1536]{1,0:T(8,128)(2,1)} %get-tuple-element.211.rest_9_), channel_id=1, source_target_pairs={{1,0},{2,1},{3,2},{7,3},{6,7},{5,6},{4,5},{0,4},{9,8},{10,9},{11,1... | collective-permute-start | bytes 1179656 | tf_op jit(solution)/shard_map/ppermute | solution.py:268
  126.6 20.6 %collective-permute-start.34 = (bf16[128,1536]{1,0:T(8,128)(2,1)}, bf16[128,1536]{1,0:T(8,128)(2,1)S(1)}, u32[]{:S(2)}, u32[]{:S(2)}) collective-permute-start(bf16[128,1536]{1,0:T(8,128)(2,1)} %get-tuple-element.212.rest_8_), channel_id=1, source_target_pairs={{0,1},{1,2},{2,3},{3,7},{7,6},{6,5},{5,4},{4,0},{8,9},{9,10},{10,1... | collective-permute-start | bytes 1179656 | tf_op jit(solution)/shard_map/ppermute | solution.py:269
  147.7 16.7 %collective-permute-start.37 = (bf16[128,1536]{1,0:T(8,128)(2,1)S(1)}, bf16[128,1536]{1,0:T(8,128)(2,1)S(1)}, u32[]{:S(2)}, u32[]{:S(2)}) collective-permute-start(bf16[128,1536]{1,0:T(8,128)(2,1)S(1)} %get-tuple-element.217.rest_25_), channel_id=1, source_target_pairs={{1,0},{2,1},{3,2},{7,3},{6,7},{5,6},{4,5},{0,4},{9,8},{10,9},{11,1... | collective-permute-start | bytes 1179656 | tf_op jit(solution)/shard_map/ppermute | solution.py:268
  147.8 17.2 %collective-permute-start.38 = (bf16[128,1536]{1,0:T(8,128)(2,1)S(1)}, bf16[128,1536]{1,0:T(8,128)(2,1)S(1)}, u32[]{:S(2)}, u32[]{:S(2)}) collective-permute-start(bf16[128,1536]{1,0:T(8,128)(2,1)S(1)} %get-tuple-element.218.rest_24_), channel_id=1, source_target_pairs={{0,1},{1,2},{2,3},{3,7},{7,6},{6,5},{5,4},{4,0},{8,9},{9,10},{10,1... | collective-permute-start | bytes 1179656 | tf_op jit(solution)/shard_map/ppermute | solution.py:269
  157.0 22.7 %collective-permute-start.40 = (bf16[128,1536]{1,0:T(8,128)(2,1)S(1)}, bf16[128,1536]{1,0:T(8,128)(2,1)S(1)}, u32[]{:S(2)}, u32[]{:S(2)}) collective-permute-start(bf16[128,1536]{1,0:T(8,128)(2,1)S(1)} %get-tuple-element.222.rest_1_), channel_id=1, source_target_pairs={{1,0},{2,1},{3,2},{7,3},{6,7},{5,6},{4,5},{0,4},{9,8},{10,9},{11,1... | collective-permute-start | bytes 1179656 | tf_op jit(solution)/shard_map/ppermute | solution.py:268
  158.9 20.9 %collective-permute-start.41 = (bf16[128,1536]{1,0:T(8,128)(2,1)S(1)}, bf16[128,1536]{1,0:T(8,128)(2,1)S(1)}, u32[]{:S(2)}, u32[]{:S(2)}) collective-permute-start(bf16[128,1536]{1,0:T(8,128)(2,1)S(1)} %get-tuple-element.223.rest_0_), channel_id=1, source_target_pairs={{0,1},{1,2},{2,3},{3,7},{7,6},{6,5},{5,4},{4,0},{8,9},{9,10},{10,1... | collective-permute-start | bytes 1179656 | tf_op jit(solution)/shard_map/ppermute | solution.py:269
  165.5 15.8 %collective-permute-start.42 = (bf16[128,1536]{1,0:T(8,128)(2,1)S(1)}, bf16[128,1536]{1,0:T(8,128)(2,1)S(1)}, u32[]{:S(2)}, u32[]{:S(2)}) collective-permute-start(bf16[128,1536]{1,0:T(8,128)(2,1)S(1)} %get-tuple-element.225.rest_9_), channel_id=1, source_target_pairs={{1,0},{2,1},{3,2},{7,3},{6,7},{5,6},{4,5},{0,4},{9,8},{10,9},{11,1... | collective-permute-start | bytes 1179656 | tf_op jit(solution)/shard_map/ppermute | solution.py:268
  193.7 18.7 %collective-permute-start.55 = (bf16[128,512]{1,0:T(8,128)(2,1)S(1)}, bf16[128,512]{1,0:T(8,128)(2,1)S(1)}, u32[]{:S(2)}, u32[]{:S(2)}) collective-permute-start(bf16[128,512]{1,0:T(8,128)(2,1)S(1)} %collective-permute-done.51.rest_14_.rest_28_), channel_id=1, source_target_pairs={{0,1},{1,2},{2,3},{3,7},{7,6},{6,5},{5,4},{4,0},{8,9},{9,10},{10,1... | collective-permute-start | bytes 393224 | tf_op jit(solution)/shard_map/ppermute | solution.py:269
  196.2 16.3 %collective-permute-start.56 = (bf16[128,512]{1,0:T(8,128)(2,1)S(1)}, bf16[128,512]{1,0:T(8,128)(2,1)S(1)}, u32[]{:S(2)}, u32[]{:S(2)}) collective-permute-start(bf16[128,512]{1,0:T(8,128)(2,1)S(1)} %collective-permute-done.52.rest_15_.rest_29_), channel_id=1, source_target_pairs={{1,0},{2,1},{3,2},{7,3},{6,7},{5,6},{4,5},{0,4},{9,8},{10,9},{11,1... | collective-permute-start | bytes 393224 | tf_op jit(solution)/shard_map/ppermute | solution.py:268
  196.9 15.6 %collective-permute-start.53 = (bf16[128,512]{1,0:T(8,128)(2,1)S(1)}, bf16[128,512]{1,0:T(8,128)(2,1)S(1)}, u32[]{:S(2)}, u32[]{:S(2)}) collective-permute-start(bf16[128,512]{1,0:T(8,128)(2,1)S(1)} %collective-permute-done.49.rest_6_.rest_20_), channel_id=1, source_target_pairs={{0,1},{1,2},{2,3},{3,7},{7,6},{6,5},{5,4},{4,0},{8,9},{9,10},{10,1... | collective-permute-start | bytes 393224 | tf_op jit(solution)/shard_map/ppermute | solution.py:269
  199.5 27.3 %collective-permute-start.39 = (bf16[128,2048]{1,0:T(8,128)(2,1)}, bf16[128,2048]{1,0:T(8,128)(2,1)S(1)}, u32[]{:S(2)}, u32[]{:S(2)}) collective-permute-start(bf16[128,2048]{1,0:T(8,128)(2,1)} %get-tuple-element.220), channel_id=1, source_target_pairs={{0,8},{4,12},{8,0},{12,4},{1,9},{5,13},{9,1},{13,5},{2,10},{6,14},... | collective-permute-start | bytes 1572872 | tf_op jit(solution)/shard_map/ppermute | solution.py:281
  (113 other events, 1401.9 us)
